TPU v7x, 256 devices: a whole 4x4x8 slice. The times are simulated.
256 devices in a mesh: pair: 8 (over z), slab: 32 (over x, y, core).
Axes of the slice: x: 4, y: 4, z: 8, core: 2. Of those that a mesh axis runs over, the one named last changes fastest.
Arguments:
- amplitudes: float32 [2048, 98304], P('pair', 'slab'), may hold values from -6 to 6
- integrals: float32 [4096, 98304], P(None, ('slab', 'pair')), may hold values from -0.078125 to 0.078125
- driver: float32 [2048, 4096], P('pair', 'slab'), may hold values from -6 to 6
- block_sizes: int32 [8], replicated, may hold values from 1 to 12288, 61440 in all
- pair_first: int32 [2048], P('pair'), may hold values from 0 to 99
- pair_second: int32 [2048], P('pair'), may hold values from 0 to 99
- ab_first: int32 [4096], P('slab'), may hold values from 0 to 999
- ab_second: int32 [4096], P('slab'), may hold values from 0 to 999
- occ_energy: float32 [100], replicated, may hold values from -2 to -0.5
- virt_energy: float32 [1000], replicated, may hold values from 0.3 to 3
Outputs:
- new_amplitudes: float32 [2048, 4096], P('pair', 'slab')
Inputs may be any that keep to these rules, and one draw needn't show every extreme that they name: `block_sizes`: the largest block holds exactly 12288 live pairs; the sizes sum to 61440.
All inputs are finite; a program needn't handle non-finite values.
Results may differ from a plain program's by a relative error of at most 0.00011.
Values sent between devices are 32-bit elements; how exact they have to be, the bound alone decides.
A program may use at most 128 MiB of HBM per device.

v0:
```python
import jax
import jax.numpy as jnp
from jax import lax
from jax.sharding import PartitionSpec as P

CAP = 12288


def lookup(table, indices):
    entries = jnp.arange(table.shape[0], dtype=jnp.int32)
    hits = indices[:, None] == entries[None, :]
    return jnp.sum(jnp.where(hits, table[None, :], jnp.zeros((), table.dtype)), axis=1)


def body(
    amplitudes,
    integrals,
    driver,
    block_sizes,
    pair_first,
    pair_second,
    ab_first,
    ab_second,
    occ_energy,
    virt_energy,
):
    columns = lax.all_to_all(amplitudes, "pair", split_axis=1, concat_axis=0, tiled=True)
    width = columns.shape[1]
    start = (lax.axis_index("slab") * lax.axis_size("pair") + lax.axis_index("pair")) * width
    column = start + jnp.arange(width, dtype=jnp.int32)
    irreps = jnp.arange(block_sizes.shape[0], dtype=jnp.int32)
    owner = (column // CAP)[:, None] == irreps[None, :]
    limit = jnp.sum(jnp.where(owner, block_sizes[None, :], 0), axis=1)
    live = column % CAP < limit
    masked = jnp.where(live[None, :], columns, jnp.zeros((), columns.dtype))
    partial_sum = lax.dot_general(
        masked,
        integrals,
        (((1,), (1,)), ((), ())),
        precision=lax.Precision.HIGHEST,
        preferred_element_type=jnp.float32,
    )
    by_slab = lax.psum_scatter(partial_sum, "slab", scatter_dimension=1, tiled=True)
    ladder = lax.psum_scatter(by_slab, "pair", scatter_dimension=0, tiled=True)
    occupied = lookup(occ_energy, pair_first) + lookup(occ_energy, pair_second)
    denominator = (
        occupied[:, None]
        - lookup(virt_energy, ab_first)[None, :]
        - lookup(virt_energy, ab_second)[None, :]
    )
    return (driver + ladder) / denominator


def solution(mesh):
    placed = (
        P("pair", "slab"),
        P(None, ("slab", "pair")),
        P("pair", "slab"),
        P(),
        P("pair"),
        P("pair"),
        P("slab"),
        P("slab"),
        P(),
        P(),
    )
    return jax.shard_map(
        body, mesh=mesh, in_specs=placed, out_specs=P("pair", "slab"), check_vma=False
    )
```

profile of v0, /device:TPU:2, one launch (start us, length us, event | category | flops | bytes accessed | tf_op | source)
XLA Modules:
  0.0 373.8 jit_solution(1860443555712645761)
XLA Ops:
  6.5 3.5 copy.13
  10.1 0.0 copy-start.4
  10.1 8.6 %all-to-all-start = ((f32[256,8,384]{0,2,1:T(8,128)}), f32[256,8,384]{0,2,1:T(8,128)S(1)}, u32[]{:S(2)}, u32[]{:S(2)}) async-start(f32[256,8,384]{0,2,1:T(8,128)} %bitcast.7), calls=%async_computation | async-start | bytes 6291456 | tf_op jit(solution)/shard_map/all_to_all | solution.py:27
  18.7 0.0 reduce-scatter.3.cloned.1.call-start
  18.8 0.0 copy-done.4
  18.8 0.1 select_reduce_fusion.4
  18.9 73.6 %all-to-all-done = f32[256,8,384]{0,2,1:T(8,128)S(1)} async-done(((f32[256,8,384]{0,2,1:T(8,128)}), f32[256,8,384]{0,2,1:T(8,128)S(1)}, u32[]{:S(2)}, u32[]{:S(2)}) %all-to-all-start) | async-done | bytes 3145760 | tf_op jit(solution)/shard_map/all_to_all | solution.py:27
  92.5 2.4 copy.14
  94.8 2.1 bitcast_select_fusion
  96.9 58.3 %fusion.6 = f32[2048,4096]{1,0:T(8,128)} fusion(f32[2048,384]{1,0:T(8,128)S(1)} %bitcast_select_fusion, f32[4096,384]{1,0:T(8,128)} %param.11), kind=kOutput, calls=%fused_computation.22 | convolution fusion | flops 38654705664 | bytes 42991616 | tf_op jit(solution)/shard_map/dot_general | solution.py:36
  155.2 0.0 copy-start.2
  155.3 0.0 copy-start.3
  155.3 0.0 copy-start.5
  155.3 0.0 copy-start.1
  155.3 0.0 copy-start.6
  155.3 0.0 copy-start.7
  155.3 0.0 copy-start
  155.3 0.0 reduce-scatter.3.cloned.1.call-update
  155.3 0.0 reduce-scatter.5.cloned.1.call-start
  155.4 168.7 %reduce-scatter.3.cloned.1.call-done = f32[2048,128]{1,0:T(8,128)} async-done(((f32[2048,4096]{1,0:T(8,128)}), f32[2048,128]{1,0:T(8,128)}) %reduce-scatter.3.cloned.1.call-update) | async-done | bytes 1048592 | tf_op jit(solution)/shard_map/reduce_scatter | solution.py:43
  324.1 0.0 reduce-scatter.5.cloned.1.call-update
  324.1 0.0 copy-done.2
  324.1 0.0 copy-done.3
  324.2 0.0 copy-done.5
  324.2 0.1 select_reduce_fusion.2
  324.3 0.0 copy-done.1
  324.3 0.0 copy-done.6
  324.3 0.0 copy-done.7
  324.3 0.2 select_reduce_fusion.1
  324.5 40.8 %reduce-scatter.5.cloned.1.call-done = f32[256,128]{1,0:T(8,128)} async-done(((f32[2048,128]{1,0:T(8,128)}), f32[256,128]{1,0:T(8,128)}) %reduce-scatter.5.cloned.1.call-update) | async-done | bytes 131088 | tf_op jit(solution)/shard_map/reduce_scatter | solution.py:44
  365.3 0.0 copy-done
  365.3 1.7 subtract_divide_fusion
  (3 shorter events, 0.0 us)
Async XLA Ops:
  10.1 8.7 %copy-start.4 = (s32[8]{0:T(128)S(1)}, s32[8]{0:T(128)}, u32[]{:S(2)}) copy-start(s32[8]{0:T(128)} %param.13) | copy-start | bytes 100
  10.1 82.4 %all-to-all-start = ((f32[256,8,384]{0,2,1:T(8,128)}), f32[256,8,384]{0,2,1:T(8,128)S(1)}, u32[]{:S(2)}, u32[]{:S(2)}) async-start(f32[256,8,384]{0,2,1:T(8,128)} %bitcast.7), calls=%async_computation | async-start | bytes 6291456 | tf_op jit(solution)/shard_map/all_to_all | solution.py:27
  18.7 305.4 %reduce-scatter.3.cloned.1.call-start = ((), (), s32[]{:S(2)}) async-start(), calls=%async_computation.3 | async-start | bytes 34603008 | tf_op jit(solution)/shard_map/reduce_scatter | solution.py:43
  155.2 168.9 %copy-start.2 = (s32[256]{0:T(256)S(1)}, s32[256]{0:T(256)}, u32[]{:S(2)}) copy-start(s32[256]{0:T(256)} %param.15) | copy-start | bytes 3076
  155.3 168.9 %copy-start.3 = (s32[256]{0:T(256)S(1)}, s32[256]{0:T(256)}, u32[]{:S(2)}) copy-start(s32[256]{0:T(256)} %param.14) | copy-start | bytes 3076
  155.3 168.9 %copy-start.5 = (f32[100]{0:T(128)S(1)}, f32[100]{0:T(128)}, u32[]{:S(2)}) copy-start(f32[100]{0:T(128)} %param.18) | copy-start | bytes 1204
  155.3 169.0 %copy-start.1 = (f32[1000]{0:T(1024)S(1)}, f32[1000]{0:T(1024)}, u32[]{:S(2)}) copy-start(f32[1000]{0:T(1024)} %param.19) | copy-start | bytes 12004
  155.3 169.0 %copy-start.6 = (s32[128]{0:T(128)S(1)}, s32[128]{0:T(128)}, u32[]{:S(2)}) copy-start(s32[128]{0:T(128)} %param.16) | copy-start | bytes 1540
  155.3 169.0 %copy-start.7 = (s32[128]{0:T(128)S(1)}, s32[128]{0:T(128)}, u32[]{:S(2)}) copy-start(s32[128]{0:T(128)} %param.17) | copy-start | bytes 1540
  155.3 210.0 %copy-start = (f32[256,128]{1,0:T(8,128)S(1)}, f32[256,128]{1,0:T(8,128)}, u32[]{:S(2)}) copy-start(f32[256,128]{1,0:T(8,128)} %param.12) | copy-start | bytes 393220
  155.3 210.0 %reduce-scatter.5.cloned.1.call-start = ((), (), s32[]{:S(2)}) async-start(), calls=%async_computation.4 | async-start | bytes 1179648 | tf_op jit(solution)/shard_map/reduce_scatter | solution.py:44
Sparse Core Ops, SparseCore 0:
  155.4 168.6 reduce-scatter.2
  326.8 38.4 reduce-scatter.4
where the time goes:
time: 374 us
  waiting for transfers between devices  283 us (76%)
  matrix products  58.3 us (16%)
  between operations  13.5 us (4%)
  starting transfers between devices  8.67 us (2%)
  local copies, waits for them, and re-layouts  5.94 us (2%)
  other arithmetic  4.2 us (1%)
    reduce_scatter x1, waiting for transfers between devices, body(): lax.psum_scatter(partial_sum, 'slab', scatter_dimension=1, tiled=True)  169 us
    all_to_all x1, waiting for transfers between devices, body(): lax.all_to_all(amplitudes, 'pair', split_axis=1, concat_axis=0, tiled=True)  73.6 us
    dot_general x1, matrix products, body(): lax.dot_general(masked, integrals, (((1,), (1,)), ((), ())), precision=la...  58.3 us
    reduce_scatter x1, waiting for transfers between devices, body(): ladder = lax.psum_scatter(by_slab, 'pair', scatter_dimension=0, tiled=True)  40.8 us
    all_to_all x1, starting transfers between devices, body(): lax.all_to_all(amplitudes, 'pair', split_axis=1, concat_axis=0, tiled=True)  8.6 us
  transfers between devices with their start and end apart: 3, of which 3 were waited for; matrix products, arithmetic and copies ran while one was open for 0% of the time, Pallas kernels for 0%

commit v1 on v0

v1 whole, which is shorter than its diff:
```python
import functools

import jax
import jax.numpy as jnp
from jax import lax
from jax.experimental import pallas as pl
from jax.experimental.pallas import tpu as pltpu
from jax.sharding import PartitionSpec as P

MESH = pl.DeviceIdType.MESH
NT = (((1,), (1,)), ((), ()))

NZ = 8
NX = 4
ROWS = 256
KD = 384
COLS = 128
SUB = 64
PER = COLS // SUB
QUART = SUB // 2
STEPS = NZ * PER
LANES = 128
MROWS = 2 * NX * SUB
RING = 4
A_BEGIN = ((0, (3, 4)), (PER, (5, 6)))
LEG1_BEGIN = 2 * PER
LEG2_BEGIN = 9 * PER // 2
Z_BEGIN = 6 * PER
ORDER = (0, 1, 7, 2, 6, 3, 5, 4)


def split(v):
    hi = v.astype(jnp.bfloat16)
    lo = (v - hi.astype(jnp.float32)).astype(jnp.bfloat16)
    return hi, lo


def ladder_kernel(
    sizes, a_hbm, b_hbm, out,
    a_own, a_sib, relay, b_own, b_sib, a3, b3, part, quad, done,
    r1, r2, r3, r4, zr,
    loc_sem, bl, bs, br, as_, ar, hs, hr, fs, fr, s1, q1, s2, q2, s3, q3, s4, q4, zs, zq,
):
    z = lax.axis_index("pair")
    s = lax.axis_index("slab")
    x, y, c = s // (2 * NX), (s // 2) % NX, s % 2

    def slab(xx, yy, cc):
        return (xx * NX + yy) * 2 + cc

    def up(v, n, d):
        return lax.rem(v + d, n)

    xp, xo, xm = up(x, NX, 1), up(x, NX, 2), up(x, NX, 3)
    yp, yo, ym = up(y, NX, 1), up(y, NX, 2), up(y, NX, 3)
    sibling = (z, slab(x, y, 1 - c))
    side = ((z, slab(xp, y, c)), (z, slab(xm, y, c)), (z, slab(x, yp, c)), (z, slab(x, ym, c)))

    def zdev(d):
        return (up(z, NZ, d), s)

    def remote(src, dst, send, recv, dev):
        return pltpu.make_async_remote_copy(
            src_ref=src, dst_ref=dst, send_sem=send, recv_sem=recv, device_id=dev, device_id_type=MESH
        )

    barrier = pltpu.get_barrier_semaphore()
    peers = [sibling, *side] + [zdev(d) for d in range(1, NZ)]
    for dev in peers:
        pl.semaphore_signal(barrier, inc=1, device_id=dev, device_id_type=MESH)
    pl.semaphore_wait(barrier, len(peers))

    def acols(d):
        return pl.ds(pl.multiple_of(up(z, NZ, d) * KD, KD), KD)

    def b_load(h):
        return pltpu.make_async_copy(b_hbm.at[:, c, pl.ds(h * SUB, SUB)], b_own.at[h], bl.at[h])

    def b_swap(h):
        return remote(b_hbm.at[:, 1 - c, pl.ds(h * SUB, SUB)], b_sib.at[h], bs.at[h], br.at[h], sibling)

    a_loc = pltpu.make_async_copy(a_hbm.at[:, acols(0)], a_own.at[0], loc_sem)
    a_swap = remote(a_hbm.at[:, acols(0)], a_sib.at[0], fs.at[0], fr.at[0], sibling)
    b_swap(0).start()
    b_load(0).start()
    a_swap.start()
    a_loc.start()
    for h in range(1, PER):
        b_swap(h).start()
        b_load(h).start()

    def a_send(k):
        d = NZ - ORDER[k]
        return remote(a_hbm.at[:, acols(d)], a_own.at[k], as_.at[k], ar.at[k], zdev(d))

    def leg1(h):
        rows = pl.ds(h * (ROWS // 2), ROWS // 2)
        return remote(a_hbm.at[rows, acols(4)], relay.at[h], hs.at[h], hr.at[h], zdev((2, 6)[h]))

    def leg2(h):
        rows = pl.ds(h * (ROWS // 2), ROWS // 2)
        return remote(relay.at[h], a_own.at[NZ - 1, rows], hs.at[2 + h], hr.at[2 + h], zdev((2, 6)[h]))

    def forward(k):
        return remote(a_own.at[k], a_sib.at[k], fs.at[k], fr.at[k], sibling)

    for k in (1, 2):
        a_send(k).start()

    limit = sizes[s // 4]
    column = lax.broadcasted_iota(jnp.int32, (SUB, KD), 1)

    def convert(src, h, first, slab_at):
        live = column < limit - (slab_at % 4) * (NZ * KD) - z * KD

        def one(j, carry):
            hi, lo = split(jnp.where(live, src[h, j], 0.0))
            rows = pl.ds(pl.multiple_of(j * SUB, SUB), SUB)
            b3[h, rows, pl.ds(first, KD)] = hi
            b3[h, rows, pl.ds(2 * KD + first, KD)] = lo
            b3[h, rows, pl.ds(4 * KD + first, KD)] = hi
            return carry

        lax.fori_loop(0, NX * NX, one, 0)

    def send1(i):
        p = lax.rem(i, RING)
        src = (
            part.at[p, 0, xo, :, pl.ds(0, QUART)],
            part.at[p, 0, xo, :, pl.ds(QUART, QUART)],
            part.at[p, 1, :, yo, pl.ds(0, QUART)],
            part.at[p, 1, :, yo, pl.ds(QUART, QUART)],
        )
        return [remote(src[k], r1.at[p, k], s1.at[p, k], q1.at[p, k], side[k]) for k in range(4)]

    def send2(i):
        p = lax.rem(i, RING)
        src = (part.at[p, 0, xp], part.at[p, 0, xm], part.at[p, 1, :, yp], part.at[p, 1, :, ym])
        return [remote(src[k], r2.at[p, k], s2.at[p, k], q2.at[p, k], side[k]) for k in range(4)]

    def send3(i):
        p = lax.rem(i, RING)
        src = (
            quad.at[p, 1, xo, pl.ds(0, QUART)],
            quad.at[p, 1, xo, pl.ds(QUART, QUART)],
            quad.at[p, 0, yo, pl.ds(0, QUART)],
            quad.at[p, 0, yo, pl.ds(QUART, QUART)],
        )
        return [remote(src[k], r3.at[p, k], s3.at[p, k], q3.at[p, k], side[k]) for k in range(4)]

    def send4(i):
        p = lax.rem(i, RING)
        src = (quad.at[p, 1, xp], quad.at[p, 1, xm], quad.at[p, 0, yp], quad.at[p, 0, ym])
        return [remote(src[k], r4.at[p, k], s4.at[p, k], q4.at[p, k], side[k]) for k in range(4)]

    def zsend(i):
        k, h = i // PER, lax.rem(i, PER)
        d = jnp.where(lax.rem(k, 2) == 1, (k + 1) // 2, NZ - k // 2)
        return remote(done.at[i], zr.at[k, h], zs.at[i], zq.at[i], zdev(d))

    def stage1(i):
        p = lax.rem(i, RING)
        k = i // PER
        h = lax.rem(i, PER)

        for step_at in range(PER):
            @pl.when(i == step_at)
            def _():
                b_load(step_at).wait()
                convert(b_own, step_at, 0, s)
                if step_at == 0:
                    a_loc.wait()
                b_swap(step_at).wait()
                convert(b_sib, step_at, KD, slab(x, y, 1 - c))

        @pl.when(h == 0)
        def _():
            forward(k).wait_recv()
            for first, source in ((0, a_own), (KD, a_sib)):
                hi, lo = split(source[k])
                a3[:, pl.ds(first, KD)] = hi
                a3[:, pl.ds(2 * KD + first, KD)] = hi
                a3[:, pl.ds(4 * KD + first, KD)] = lo

        def columns(m, carry):
            rows = pl.ds(pl.multiple_of(m * MROWS, MROWS), MROWS)
            acc = lax.dot_general(b3[h, rows, :], a3[...], NT, preferred_element_type=jnp.float32)
            for xx in range(2):
                for yy in range(NX):
                    at = (xx * NX + yy) * SUB
                    for half in range(2):
                        part[p, half, 2 * m + xx, yy] = acc[at:at + SUB, half * LANES:(half + 1) * LANES]
            return carry

        lax.fori_loop(0, NX // 2, columns, 0)
        for copy in send1(i):
            copy.start()

        for begin, blocks in A_BEGIN:
            @pl.when(i == begin)
            def _():
                for kk in blocks:
                    a_send(kk).start()

        @pl.when(i == LEG1_BEGIN)
        def _():
            for half in range(2):
                leg1(half).start()

        @pl.when(i == LEG2_BEGIN)
        def _():
            for half in range(2):
                leg1(half).wait_recv()
                leg2(half).start()

    def fetch(i):
        k = i // PER

        @pl.when(k < NZ - 2)
        def _():
            a_wait = remote(a_own.at[k + 1], a_own.at[k + 1], as_.at[k + 1], ar.at[k + 1], sibling)
            a_wait.wait_recv()
            forward(k + 1).start()

        @pl.when(k == NZ - 2)
        def _():
            for half in range(2):
                leg2(half).wait_recv()
            forward(NZ - 1).start()

    def stage2(i):
        p = lax.rem(i, RING)
        for copy in send1(i):
            copy.wait()
        part[p, 0, xp, :, pl.ds(0, QUART)] += r1[p, 0]
        part[p, 0, xm, :, pl.ds(QUART, QUART)] += r1[p, 1]
        part[p, 1, :, yp, pl.ds(0, QUART)] += r1[p, 2]
        part[p, 1, :, ym, pl.ds(QUART, QUART)] += r1[p, 3]
        for copy in send2(i):
            copy.start()

    def stage3(i):
        p = lax.rem(i, RING)
        for copy in send2(i):
            copy.wait()
        quad[p, 0] = part[p, 0, x] + (r2[p, 0] + r2[p, 1])
        quad[p, 1] = part[p, 1, :, y] + (r2[p, 2] + r2[p, 3])
        for copy in send3(i):
            copy.start()

    def stage4(i):
        p = lax.rem(i, RING)
        for copy in send3(i):
            copy.wait()
        quad[p, 1, xp, pl.ds(0, QUART)] += r3[p, 0]
        quad[p, 1, xm, pl.ds(QUART, QUART)] += r3[p, 1]
        quad[p, 0, yp, pl.ds(0, QUART)] += r3[p, 2]
        quad[p, 0, ym, pl.ds(QUART, QUART)] += r3[p, 3]
        for copy in send4(i):
            copy.start()

    def stage5(i):
        p = lax.rem(i, RING)
        for copy in send4(i):
            copy.wait()
        done[i, :, pl.ds(0, LANES)] = quad[p, 0, y] + (r4[p, 2] + r4[p, 3])
        done[i, :, pl.ds(LANES, LANES)] = quad[p, 1, x] + (r4[p, 0] + r4[p, 1])

        @pl.when(i > Z_BEGIN - 4)
        def _():
            zsend(i).start()

    def step(i, carry):
        pl.when(jnp.logical_and(lax.rem(i, PER) == PER - 1, i < STEPS - PER))(functools.partial(fetch, i))
        for lag, stage in enumerate((stage1, stage2, stage3, stage4, stage5)):
            pl.when(jnp.logical_and(i >= lag, i < STEPS + lag))(functools.partial(stage, i - lag))

        @pl.when(i == Z_BEGIN)
        def _():
            def begin(j, carry):
                zsend(j).start()
                return carry

            lax.fori_loop(PER, Z_BEGIN - 3, begin, 0)

        return carry

    lax.fori_loop(0, STEPS + 4, step, 0)

    def gather(i, carry):
        zsend(i).wait()
        h = lax.rem(i, PER)
        done[h] += zr[i // PER, h]
        return carry

    lax.fori_loop(PER, STEPS, gather, 0)
    for h in range(PER):
        out[:, pl.ds(h * SUB, SUB)] = done[h].T
    a_swap.wait_send()
    for k in range(1, NZ):
        forward(k).wait_send()
    for k in range(1, NZ - 1):
        a_send(k).wait_send()
    for half in range(2):
        leg1(half).wait_send()
        leg2(half).wait_send()


def ladder_of(amplitudes, integrals, block_sizes):
    f32, bf16 = jnp.float32, jnp.bfloat16
    dma = pltpu.SemaphoreType.DMA
    scratch = [
        pltpu.VMEM((NZ, ROWS, KD), f32),
        pltpu.VMEM((NZ, ROWS, KD), f32),
        pltpu.VMEM((2, ROWS // 2, KD), f32),
        pltpu.VMEM((PER, NX * NX, SUB, KD), f32),
        pltpu.VMEM((PER, NX * NX, SUB, KD), f32),
        pltpu.VMEM((ROWS, 6 * KD), bf16),
        pltpu.VMEM((PER, NX * NX * SUB, 6 * KD), bf16),
        pltpu.VMEM((RING, 2, NX, NX, SUB, LANES), f32),
        pltpu.VMEM((RING, 2, NX, SUB, LANES), f32),
        pltpu.VMEM((STEPS, SUB, ROWS), f32),
        pltpu.VMEM((RING, 4, NX, QUART, LANES), f32),
        pltpu.VMEM((RING, 4, NX, SUB, LANES), f32),
        pltpu.VMEM((RING, 4, QUART, LANES), f32),
        pltpu.VMEM((RING, 4, SUB, LANES), f32),
        pltpu.VMEM((NZ, PER, SUB, ROWS), f32),
        dma, dma((PER,)), dma((PER,)), dma((PER,)),
        dma((NZ,)), dma((NZ,)), dma((4,)), dma((4,)), dma((NZ,)), dma((NZ,)),
        dma((RING, 4)), dma((RING, 4)), dma((RING, 4)), dma((RING, 4)),
        dma((RING, 4)), dma((RING, 4)), dma((RING, 4)), dma((RING, 4)),
        dma((STEPS,)), dma((STEPS,)),
    ]
    return pl.pallas_call(
        ladder_kernel,
        out_shape=jax.ShapeDtypeStruct((ROWS, COLS), f32),
        in_specs=[
            pl.BlockSpec(memory_space=pltpu.SMEM),
            pl.BlockSpec(memory_space=pl.ANY),
            pl.BlockSpec(memory_space=pl.ANY),
        ],
        out_specs=pl.BlockSpec(memory_space=pltpu.VMEM),
        scratch_shapes=scratch,
        compiler_params=pltpu.CompilerParams(
            collective_id=0, has_side_effects=True, vmem_limit_bytes=52 * 1024 * 1024
        ),
        cost_estimate=pl.CostEstimate(
            flops=3 * 2 * 2048 * 2048 * 768, bytes_accessed=12 * 1024 * 1024, transcendentals=0
        ),
        name="ladder",
    )(block_sizes, amplitudes, integrals.reshape(NX * NX, 2, COLS, KD))


def lookup(table, indices):
    entries = jnp.arange(table.shape[0], dtype=jnp.int32)
    hits = indices[:, None] == entries[None, :]
    return jnp.sum(jnp.where(hits, table[None, :], jnp.zeros((), table.dtype)), axis=1)


def body(
    amplitudes,
    integrals,
    driver,
    block_sizes,
    pair_first,
    pair_second,
    ab_first,
    ab_second,
    occ_energy,
    virt_energy,
):
    ladder = ladder_of(amplitudes, integrals, block_sizes)
    occupied = lookup(occ_energy, pair_first) + lookup(occ_energy, pair_second)
    denominator = (
        occupied[:, None]
        - lookup(virt_energy, ab_first)[None, :]
        - lookup(virt_energy, ab_second)[None, :]
    )
    return (driver + ladder) / denominator


def solution(mesh):
    placed = (
        P("pair", "slab"),
        P(None, ("slab", "pair")),
        P("pair", "slab"),
        P(),
        P("pair"),
        P("pair"),
        P("slab"),
        P("slab"),
        P(),
        P(),
    )
    return jax.shard_map(
        body, mesh=mesh, in_specs=placed, out_specs=P("pair", "slab"), check_vma=False
    )
```

time: 374 us -> 130 us (0.35)
  waiting for transfers between devices: 283 us -> 0 us
  Pallas kernels: 0 us -> 124 us
  matrix products: 58.3 us -> 0 us
  between operations: 13.5 us -> 0.04 us
  starting transfers between devices: 8.67 us -> 0 us
  local copies, waits for them, and re-layouts: 5.94 us -> 0.65 us
    reduce_scatter x2 -> x0, waiting for transfers between devices: 210 us -> none  [the longest x1 169 us: body(): lax.psum_scatter(partial_sum, 'slab', scatter_dimension=1, tiled=True)]
    pallas_call x0 -> x1, Pallas kernels: none -> 124 us  [ladder_of(): pl.pallas_call(ladder_kernel, out_shape=jax.ShapeDtypeStruct((ROWS, COLS)...]
    all_to_all x1 -> x0, waiting for transfers between devices: 73.6 us -> none  [body(): lax.all_to_all(amplitudes, 'pair', split_axis=1, concat_axis=0, tiled=True)]
    dot_general x1 -> x0, matrix products: 58.3 us -> none  [body(): lax.dot_general(masked, integrals, (((1,), (1,)), ((), ())), precision=la...]
    all_to_all x1 -> x0, starting transfers between devices: 8.6 us -> none  [body(): lax.all_to_all(amplitudes, 'pair', split_axis=1, concat_axis=0, tiled=True)]
  transfers between devices with their start and end apart: 3 -> 0, of which waited for: 3 -> 0; matrix products, arithmetic and copies ran while one was open for 0% -> 0% of each run, Pallas kernels for 0% -> 0%
where the time goes in v1:
time: 130 us; the launch traced here: 127 us
  Pallas kernels  124 us (95%)
  other arithmetic  2.5 us (2%)
    pallas_call x1, Pallas kernels, ladder_of(): pl.pallas_call(ladder_kernel, out_shape=jax.ShapeDtypeStruct((ROWS, COLS)...  124 us

profile of v1, /device:TPU:2, one launch (start us, length us, event | category | flops | bytes accessed | tf_op | source)
XLA Modules:
  0.0 127.4 jit_solution(500962444874199375)
XLA Ops:
  0.0 0.9 select_reduce_fusion.1
  0.9 0.8 select_reduce_fusion.2
  1.7 0.0 copy-start
  1.8 0.6 copy-done
  2.4 0.0 copy-start.1
  2.4 124.2 %ladder.1 = f32[256,128]{1,0:T(8,128)S(1)} custom-call(s32[8]{0:T(128)S(1)} %copy-done, f32[256,3072]{1,0:T(8,128)} %a_hbm.1, f32[16,2,128,384]{3,2,1,0:T(8,128)} %bitcast.1), custom_call_target="tpu_custom_call" | custom-call | flops 19327352832 | bytes 12582912 | tf_op jit(solution)/shard_map/ladder/pallas_call | solution.py:334
  126.6 0.0 copy-done.1
  126.6 0.8 subtract_divide_fusion
  (1 shorter events, 0.0 us)
Async XLA Ops:
  1.7 0.7 copy-start
  2.4 124.2 %copy-start.1 = (f32[256,128]{1,0:T(8,128)S(1)}, f32[256,128]{1,0:T(8,128)}, u32[]{:S(2)}) copy-start(f32[256,128]{1,0:T(8,128)} %param.12) | copy-start | bytes 393220

commit v2 on v1

--- a/solution.py
+++ b/solution.py
@@ -22,11 +22,14 @@
 LANES = 128
 MROWS = 2 * NX * SUB
 RING = 4
-A_BEGIN = ((0, (3, 4)), (PER, (5, 6)))
-LEG1_BEGIN = 2 * PER
-LEG2_BEGIN = 9 * PER // 2
-Z_BEGIN = 6 * PER
-ORDER = (0, 1, 7, 2, 6, 3, 5, 4)
+ORDER = (0, 7, 6, 2, 3, 5, 4, 1)
+FAR = ORDER.index(4)
+FIRST = (1, 2, 3)
+A_BEGIN = ((0, (4,)), (2, (5,)), (5, (7,)))
+LEG1_BEGIN = 5
+LEG2_BEGIN = 8
+Z_BEGIN = 14
+Z_END = STEPS + 2
 
 
 def split(v):
@@ -36,10 +39,10 @@
 
 
 def ladder_kernel(
-    sizes, a_hbm, b_hbm, out,
-    a_own, a_sib, relay, b_own, b_sib, a3, b3, part, quad, done,
-    r1, r2, r3, r4, zr,
-    loc_sem, bl, bs, br, as_, ar, hs, hr, fs, fr, s1, q1, s2, q2, s3, q3, s4, q4, zs, zq,
+    sizes_hbm, a_hbm, b_hbm, pf_hbm, ps_hbm, af_hbm, as_hbm, occ_hbm, virt_hbm, drive_hbm, out,
+    drive, drive_sem, denominator, sizes, pf, ps, af, asec, occ, virt, small_sem, a_own, a_sib, relay, b_own, b_sib, a3, b3, part, quad, done,
+    r1, r2, r3, r4, mg, mh, fin,
+    loc_sem, bl, bs, br, as_, ar, hs, hr, fs, fr, s1, q1, s2, q2, s3, q3, s4, q4, zs, zq, es, eq,
 ):
     z = lax.axis_index("pair")
     s = lax.axis_index("slab")
@@ -69,6 +72,9 @@
     for dev in peers:
         pl.semaphore_signal(barrier, inc=1, device_id=dev, device_id_type=MESH)
     pl.semaphore_wait(barrier, len(peers))
+
+    small = ((sizes_hbm, sizes), (pf_hbm, pf), (ps_hbm, ps), (af_hbm, af), (as_hbm, asec), (occ_hbm, occ), (virt_hbm, virt))
+    small = [pltpu.make_async_copy(src, dst, small_sem.at[n]) for n, (src, dst) in enumerate(small)]
 
     def acols(d):
         return pl.ds(pl.multiple_of(up(z, NZ, d) * KD, KD), KD)
@@ -85,6 +91,8 @@
     b_load(0).start()
     a_swap.start()
     a_loc.start()
+    for copy in small:
+        copy.start()
     for h in range(1, PER):
         b_swap(h).start()
         b_load(h).start()
@@ -99,13 +107,16 @@
 
     def leg2(h):
         rows = pl.ds(h * (ROWS // 2), ROWS // 2)
-        return remote(relay.at[h], a_own.at[NZ - 1, rows], hs.at[2 + h], hr.at[2 + h], zdev((2, 6)[h]))
+        return remote(relay.at[h], a_own.at[FAR, rows], hs.at[2 + h], hr.at[2 + h], zdev((2, 6)[h]))
 
     def forward(k):
         return remote(a_own.at[k], a_sib.at[k], fs.at[k], fr.at[k], sibling)
 
-    for k in (1, 2):
+    drive_copy = pltpu.make_async_copy(drive_hbm, drive, drive_sem)
+    drive_copy.start()
+    for k in FIRST:
         a_send(k).start()
+    small[0].wait()
 
     limit = sizes[s // 4]
     column = lax.broadcasted_iota(jnp.int32, (SUB, KD), 1)
@@ -153,10 +164,42 @@
         src = (quad.at[p, 1, xp], quad.at[p, 1, xm], quad.at[p, 0, yp], quad.at[p, 0, ym])
         return [remote(src[k], r4.at[p, k], s4.at[p, k], q4.at[p, k], side[k]) for k in range(4)]
 
-    def zsend(i):
-        k, h = i // PER, lax.rem(i, PER)
-        d = jnp.where(lax.rem(k, 2) == 1, (k + 1) // 2, NZ - k // 2)
-        return remote(done.at[i], zr.at[k, h], zs.at[i], zq.at[i], zdev(d))
+    def zparts(k):
+        return range(2 if k == FAR else 1)
+
+    def zsend(k, h, part_at):
+        d, i = ORDER[k], k * PER + h
+        if d == 4:
+            src, dst, dev = done.at[i, pl.ds(part_at * QUART, QUART)], mh.at[part_at, h], zdev(3 + 2 * part_at)
+        elif d < 4:
+            src, dst, dev = done.at[i], mg.at[0, d - 2, h], zdev(d - 1)
+        else:
+            src, dst, dev = done.at[i], mg.at[1, 6 - d, h], zdev(d + 1)
+        return remote(src, dst, zs.at[k, h, part_at], zq.at[k, h, part_at], dev)
+
+    def zstart(i):
+        for k, d in enumerate(ORDER):
+            if d not in (0, 1, 7):
+                @pl.when(i // PER == k)
+                def _():
+                    for n in zparts(k):
+                        zsend(k, lax.rem(i, PER), n).start()
+
+    def last(n, h):
+        i = ORDER.index((1, 7)[n]) * PER + h
+        return remote(done.at[i], fin.at[n, h], es.at[n, h], eq.at[n, h], zdev((1, 7)[n]))
+
+    def merge(n, h):
+        for d in ((2, 3), (6, 5))[n]:
+            zsend(ORDER.index(d), h, 0).wait_recv()
+        zsend(FAR, h, n).wait_recv()
+        i = ORDER.index((1, 7)[n]) * PER + h
+        done[i] += mg[n, 0, h] + mg[n, 1, h]
+        done[i, pl.ds(n * QUART, QUART)] += mh[n, h]
+        last(n, h).start()
+
+    def ready(n, h):
+        return ORDER.index((1, 7)[n]) * PER + h + 4 <= Z_END
 
     def stage1(i):
         p = lax.rem(i, RING)
@@ -207,26 +250,20 @@
             for half in range(2):
                 leg1(half).start()
 
-        @pl.when(i == LEG2_BEGIN)
-        def _():
-            for half in range(2):
-                leg1(half).wait_recv()
-                leg2(half).start()
-
     def fetch(i):
         k = i // PER
 
-        @pl.when(k < NZ - 2)
+        @pl.when(k + 1 != FAR)
         def _():
             a_wait = remote(a_own.at[k + 1], a_own.at[k + 1], as_.at[k + 1], ar.at[k + 1], sibling)
             a_wait.wait_recv()
-            forward(k + 1).start()
-
-        @pl.when(k == NZ - 2)
+
+        @pl.when(k + 1 == FAR)
         def _():
             for half in range(2):
                 leg2(half).wait_recv()
-            forward(NZ - 1).start()
+
+        forward(k + 1).start()
 
     def stage2(i):
         p = lax.rem(i, RING)
@@ -268,48 +305,94 @@
 
         @pl.when(i > Z_BEGIN - 4)
         def _():
-            zsend(i).start()
+            zstart(i)
+
+    def looked_up(table, index, width):
+        entry = lax.broadcasted_iota(jnp.int32, (table.shape[1], width), 0)
+        hits = jnp.where(entry == index[...], 1.0, 0.0)
+        row = jnp.broadcast_to(table[...], (8, table.shape[1]))
+        return lax.dot_general(
+            row, hits, (((1,), (0,)), ((), ())), precision=lax.Precision.HIGHEST, preferred_element_type=jnp.float32
+        )[0:1]
+
+    def energies():
+        for copy in small[1:]:
+            copy.wait()
+        occupied = looked_up(occ, pf, ROWS) + looked_up(occ, ps, ROWS)
+        rows = jnp.broadcast_to(occupied, (COLS, ROWS)).T
+        first, second = looked_up(virt, af, COLS), looked_up(virt, asec, COLS)
+        denominator[...] = (rows - first) - second
 
     def step(i, carry):
         pl.when(jnp.logical_and(lax.rem(i, PER) == PER - 1, i < STEPS - PER))(functools.partial(fetch, i))
         for lag, stage in enumerate((stage1, stage2, stage3, stage4, stage5)):
             pl.when(jnp.logical_and(i >= lag, i < STEPS + lag))(functools.partial(stage, i - lag))
 
+        pl.when(i == PER)(energies)
+
+        @pl.when(i == LEG2_BEGIN)
+        def _():
+            for half in range(2):
+                leg1(half).wait_recv()
+                leg2(half).start()
+
         @pl.when(i == Z_BEGIN)
         def _():
             def begin(j, carry):
-                zsend(j).start()
+                zstart(j)
                 return carry
 
             lax.fori_loop(PER, Z_BEGIN - 3, begin, 0)
 
+        @pl.when(i == Z_END)
+        def _():
+            for n in range(2):
+                for h in range(PER):
+                    if ready(n, h):
+                        merge(n, h)
+
         return carry
 
     lax.fori_loop(0, STEPS + 4, step, 0)
 
-    def gather(i, carry):
-        zsend(i).wait()
-        h = lax.rem(i, PER)
-        done[h] += zr[i // PER, h]
-        return carry
-
-    lax.fori_loop(PER, STEPS, gather, 0)
+    for n in range(2):
+        for h in range(PER):
+            if not ready(n, h):
+                merge(n, h)
+    drive_copy.wait()
     for h in range(PER):
-        out[:, pl.ds(h * SUB, SUB)] = done[h].T
+        for n in range(2):
+            last(n, h).wait_recv()
+        cols = pl.ds(h * SUB, SUB)
+        ladder = (done[h] + (fin[0, h] + fin[1, h])).T
+        out[:, cols] = (drive[:, cols] + ladder) / denominator[:, cols]
+    for n in range(2):
+        for h in range(PER):
+            last(n, h).wait_send()
+    for k, d in enumerate(ORDER):
+        if d not in (0, 1, 7):
+            for h in range(PER):
+                for n in zparts(k):
+                    zsend(k, h, n).wait_send()
     a_swap.wait_send()
     for k in range(1, NZ):
         forward(k).wait_send()
-    for k in range(1, NZ - 1):
-        a_send(k).wait_send()
+    for k in range(1, NZ):
+        if k != FAR:
+            a_send(k).wait_send()
     for half in range(2):
         leg1(half).wait_send()
         leg2(half).wait_send()
 
 
-def ladder_of(amplitudes, integrals, block_sizes):
+def update(amplitudes, integrals, driver, block_sizes, *tables):
     f32, bf16 = jnp.float32, jnp.bfloat16
     dma = pltpu.SemaphoreType.DMA
     scratch = [
+        pltpu.VMEM((ROWS, COLS), f32), dma, pltpu.VMEM((ROWS, COLS), f32),
+        pltpu.SMEM((NZ,), jnp.int32),
+        *(pltpu.VMEM(table.shape, table.dtype) for table in tables),
+        dma((len(tables) + 1,)),
         pltpu.VMEM((NZ, ROWS, KD), f32),
         pltpu.VMEM((NZ, ROWS, KD), f32),
         pltpu.VMEM((2, ROWS // 2, KD), f32),
@@ -324,37 +407,29 @@
         pltpu.VMEM((RING, 4, NX, SUB, LANES), f32),
         pltpu.VMEM((RING, 4, QUART, LANES), f32),
         pltpu.VMEM((RING, 4, SUB, LANES), f32),
-        pltpu.VMEM((NZ, PER, SUB, ROWS), f32),
+        pltpu.VMEM((2, 2, PER, SUB, ROWS), f32),
+        pltpu.VMEM((2, PER, QUART, ROWS), f32),
+        pltpu.VMEM((2, PER, SUB, ROWS), f32),
         dma, dma((PER,)), dma((PER,)), dma((PER,)),
         dma((NZ,)), dma((NZ,)), dma((4,)), dma((4,)), dma((NZ,)), dma((NZ,)),
         dma((RING, 4)), dma((RING, 4)), dma((RING, 4)), dma((RING, 4)),
         dma((RING, 4)), dma((RING, 4)), dma((RING, 4)), dma((RING, 4)),
-        dma((STEPS,)), dma((STEPS,)),
+        dma((NZ, PER, 2)), dma((NZ, PER, 2)), dma((2, PER)), dma((2, PER)),
     ]
     return pl.pallas_call(
         ladder_kernel,
         out_shape=jax.ShapeDtypeStruct((ROWS, COLS), f32),
-        in_specs=[
-            pl.BlockSpec(memory_space=pltpu.SMEM),
-            pl.BlockSpec(memory_space=pl.ANY),
-            pl.BlockSpec(memory_space=pl.ANY),
-        ],
+        in_specs=[pl.BlockSpec(memory_space=pltpu.HBM)] * (4 + len(tables)),
         out_specs=pl.BlockSpec(memory_space=pltpu.VMEM),
         scratch_shapes=scratch,
         compiler_params=pltpu.CompilerParams(
-            collective_id=0, has_side_effects=True, vmem_limit_bytes=52 * 1024 * 1024
+            collective_id=0, has_side_effects=True, vmem_limit_bytes=60 * 1024 * 1024
         ),
         cost_estimate=pl.CostEstimate(
             flops=3 * 2 * 2048 * 2048 * 768, bytes_accessed=12 * 1024 * 1024, transcendentals=0
         ),
         name="ladder",
-    )(block_sizes, amplitudes, integrals.reshape(NX * NX, 2, COLS, KD))
-
-
-def lookup(table, indices):
-    entries = jnp.arange(table.shape[0], dtype=jnp.int32)
-    hits = indices[:, None] == entries[None, :]
-    return jnp.sum(jnp.where(hits, table[None, :], jnp.zeros((), table.dtype)), axis=1)
+    )(block_sizes, amplitudes, integrals.reshape(NX * NX, 2, COLS, KD), *tables, driver)
 
 
 def body(
@@ -369,14 +444,8 @@
     occ_energy,
     virt_energy,
 ):
-    ladder = ladder_of(amplitudes, integrals, block_sizes)
-    occupied = lookup(occ_energy, pair_first) + lookup(occ_energy, pair_second)
-    denominator = (
-        occupied[:, None]
-        - lookup(virt_energy, ab_first)[None, :]
-        - lookup(virt_energy, ab_second)[None, :]
-    )
-    return (driver + ladder) / denominator
+    tables = (pair_first, pair_second, ab_first, ab_second, occ_energy, virt_energy)
+    return update(amplitudes, integrals, driver, block_sizes, *(table[None] for table in tables))
 
 
 def solution(mesh):

time: 130 us -> 130 us (level); the launches traced: 127 us -> 130 us
  Pallas kernels: 124 us -> 128 us
  other arithmetic: 2.5 us -> 0 us
    pallas_call x1, Pallas kernels: 124 us -> 128 us  [update(): pl.pallas_call(ladder_kernel, out_shape=jax.ShapeDtypeStruct((ROWS, COLS)...]
    reduce_sum x2 -> x0, other arithmetic: 1.73 us -> none  [lookup(): jnp.sum(jnp.where(hits, table[None, :], jnp.zeros((), table.dtype)), axis=1)]
where the time goes in v2:
time: 130 us
  Pallas kernels  128 us (98%)
  local copies, waits for them, and re-layouts  1.57 us (1%)
    pallas_call x1, Pallas kernels, update(): pl.pallas_call(ladder_kernel, out_shape=jax.ShapeDtypeStruct((ROWS, COLS)...  128 us

profile of v2, /device:TPU:2, one launch (start us, length us, event | category | flops | bytes accessed | tf_op | source)
XLA Modules:
  0.0 129.5 jit_solution(7664728079325496049)
XLA Ops:
  0.0 127.9 %ladder.1 = f32[256,128]{1,0:T(8,128)} custom-call(s32[8]{0:T(128)} %sizes_hbm.1, f32[256,3072]{1,0:T(8,128)} %a_hbm.1, f32[16,2,128,384]{3,2,1,0:T(8,128)} %bitcast.7, s32[1,256]{1,0:T(1,128)} %bitcast.9, s32[1,256]{1,0:T(1,128)} %bitcast.10, s32[1,128]{1,0:T(1,128)} %bitcast.11, s32[1,128]{1,0:T(1,128)} %bitcast.12, f32[1,100]{1,0:T(1,128)} %bitcast.13, ...), custom_call_target="tpu_custom_call" | custom-call | flops 19327352832 | bytes 12582912 | tf_op jit(solution)/shard_map/ladder/pallas_call | solution.py:419
  128.0 1.6 %copy.12 = f32[256,128]{1,0:T(8,128)} copy(f32[256,128]{1,0:T(8,128)} %ladder.1) | data formatting | bytes 262144

commit v3 on v2

--- a/solution.py
+++ b/solution.py
@@ -71,7 +71,6 @@
     peers = [sibling, *side] + [zdev(d) for d in range(1, NZ)]
     for dev in peers:
         pl.semaphore_signal(barrier, inc=1, device_id=dev, device_id_type=MESH)
-    pl.semaphore_wait(barrier, len(peers))
 
     small = ((sizes_hbm, sizes), (pf_hbm, pf), (ps_hbm, ps), (af_hbm, af), (as_hbm, asec), (occ_hbm, occ), (virt_hbm, virt))
     small = [pltpu.make_async_copy(src, dst, small_sem.at[n]) for n, (src, dst) in enumerate(small)]
@@ -87,36 +86,58 @@
 
     a_loc = pltpu.make_async_copy(a_hbm.at[:, acols(0)], a_own.at[0], loc_sem)
     a_swap = remote(a_hbm.at[:, acols(0)], a_sib.at[0], fs.at[0], fr.at[0], sibling)
-    b_swap(0).start()
-    b_load(0).start()
-    a_swap.start()
-    a_loc.start()
+    drive_copy = pltpu.make_async_copy(drive_hbm, drive, drive_sem)
     for copy in small:
         copy.start()
+    b_load(0).start()
+    a_loc.start()
+    pl.semaphore_wait(barrier, len(peers))
+    b_swap(0).start()
+    a_swap.start()
+
+    def a_send(k):
+        d = NZ - ORDER[k]
+        return remote(a_hbm.at[:, acols(d)], a_own.at[k], as_.at[k], ar.at[k], zdev(d))
+
+    def leg1(h):
+        rows = pl.ds(h * (ROWS // 2), ROWS // 2)
+        return remote(a_hbm.at[rows, acols(4)], relay.at[h], hs.at[h], hr.at[h], zdev((2, 6)[h]))
+
+    def leg2(h):
+        rows = pl.ds(h * (ROWS // 2), ROWS // 2)
+        return remote(relay.at[h], a_own.at[FAR, rows], hs.at[2 + h], hr.at[2 + h], zdev((2, 6)[h]))
+
+    def forward(k):
+        return remote(a_own.at[k], a_sib.at[k], fs.at[k], fr.at[k], sibling)
+
+    for k in FIRST:
+        a_send(k).start()
     for h in range(1, PER):
         b_swap(h).start()
         b_load(h).start()
-
-    def a_send(k):
-        d = NZ - ORDER[k]
-        return remote(a_hbm.at[:, acols(d)], a_own.at[k], as_.at[k], ar.at[k], zdev(d))
-
-    def leg1(h):
-        rows = pl.ds(h * (ROWS // 2), ROWS // 2)
-        return remote(a_hbm.at[rows, acols(4)], relay.at[h], hs.at[h], hr.at[h], zdev((2, 6)[h]))
-
-    def leg2(h):
-        rows = pl.ds(h * (ROWS // 2), ROWS // 2)
-        return remote(relay.at[h], a_own.at[FAR, rows], hs.at[2 + h], hr.at[2 + h], zdev((2, 6)[h]))
-
-    def forward(k):
-        return remote(a_own.at[k], a_sib.at[k], fs.at[k], fr.at[k], sibling)
-
-    drive_copy = pltpu.make_async_copy(drive_hbm, drive, drive_sem)
     drive_copy.start()
-    for k in FIRST:
-        a_send(k).start()
     small[0].wait()
+
+    def looked_up(table, index, width):
+        entry = lax.broadcasted_iota(jnp.int32, (table.shape[1], width), 0)
+        hits = jnp.where(entry == index[...], 1.0, 0.0).astype(jnp.bfloat16)
+        row = jnp.broadcast_to(table[...], (8, table.shape[1]))
+        hi = row.astype(jnp.bfloat16).astype(jnp.float32)
+        mid = (row - hi).astype(jnp.bfloat16).astype(jnp.float32)
+        term = lax.broadcasted_iota(jnp.int32, row.shape, 0)
+        terms = jnp.where(term == 0, hi, jnp.where(term == 1, mid, row - hi - mid)).astype(jnp.bfloat16)
+        got = lax.dot_general(terms, hits, (((1,), (0,)), ((), ())), preferred_element_type=jnp.float32)
+        return got[0:1] + (got[1:2] + got[2:3])
+
+    def energies():
+        for copy in small[1:]:
+            copy.wait()
+        occupied = looked_up(occ, pf, ROWS) + looked_up(occ, ps, ROWS)
+        rows = jnp.broadcast_to(occupied, (COLS, ROWS)).T
+        first, second = looked_up(virt, af, COLS), looked_up(virt, asec, COLS)
+        denominator[...] = (rows - first) - second
+
+    energies()
 
     limit = sizes[s // 4]
     column = lax.broadcasted_iota(jnp.int32, (SUB, KD), 1)
@@ -307,28 +328,10 @@
         def _():
             zstart(i)
 
-    def looked_up(table, index, width):
-        entry = lax.broadcasted_iota(jnp.int32, (table.shape[1], width), 0)
-        hits = jnp.where(entry == index[...], 1.0, 0.0)
-        row = jnp.broadcast_to(table[...], (8, table.shape[1]))
-        return lax.dot_general(
-            row, hits, (((1,), (0,)), ((), ())), precision=lax.Precision.HIGHEST, preferred_element_type=jnp.float32
-        )[0:1]
-
-    def energies():
-        for copy in small[1:]:
-            copy.wait()
-        occupied = looked_up(occ, pf, ROWS) + looked_up(occ, ps, ROWS)
-        rows = jnp.broadcast_to(occupied, (COLS, ROWS)).T
-        first, second = looked_up(virt, af, COLS), looked_up(virt, asec, COLS)
-        denominator[...] = (rows - first) - second
-
     def step(i, carry):
         pl.when(jnp.logical_and(lax.rem(i, PER) == PER - 1, i < STEPS - PER))(functools.partial(fetch, i))
         for lag, stage in enumerate((stage1, stage2, stage3, stage4, stage5)):
             pl.when(jnp.logical_and(i >= lag, i < STEPS + lag))(functools.partial(stage, i - lag))
-
-        pl.when(i == PER)(energies)
 
         @pl.when(i == LEG2_BEGIN)
         def _():

time: 130 us -> 130 us (level)
  no operation moved by 1% of the time
where the time goes in v3:
time: 130 us
  Pallas kernels  128 us (98%)
  local copies, waits for them, and re-layouts  1.57 us (1%)
    pallas_call x1, Pallas kernels, update(): pl.pallas_call(ladder_kernel, out_shape=jax.ShapeDtypeStruct((ROWS, COLS)...  128 us

profile of v3, /device:TPU:2, one launch (start us, length us, event | category | flops | bytes accessed | tf_op | source)
XLA Modules:
  0.0 129.5 jit_solution(1169708816142614412)
XLA Ops:
  0.0 128.0 %ladder.1 = f32[256,128]{1,0:T(8,128)} custom-call(s32[8]{0:T(128)} %sizes_hbm.1, f32[256,3072]{1,0:T(8,128)} %a_hbm.1, f32[16,2,128,384]{3,2,1,0:T(8,128)} %bitcast.7, s32[1,256]{1,0:T(1,128)} %bitcast.9, s32[1,256]{1,0:T(1,128)} %bitcast.10, s32[1,128]{1,0:T(1,128)} %bitcast.11, s32[1,128]{1,0:T(1,128)} %bitcast.12, f32[1,100]{1,0:T(1,128)} %bitcast.13, ...), custom_call_target="tpu_custom_call" | custom-call | flops 19327352832 | bytes 12582912 | tf_op jit(solution)/shard_map/ladder/pallas_call | solution.py:422
  128.0 1.6 %copy.12 = f32[256,128]{1,0:T(8,128)} copy(f32[256,128]{1,0:T(8,128)} %ladder.1) | data formatting | bytes 262144

commit v4 on v3

--- a/solution.py
+++ b/solution.py
@@ -22,13 +22,13 @@
 LANES = 128
 MROWS = 2 * NX * SUB
 RING = 4
-ORDER = (0, 7, 6, 2, 3, 5, 4, 1)
+ORDER = (0, 1, 7, 2, 6, 3, 5, 4)
 FAR = ORDER.index(4)
-FIRST = (1, 2, 3)
-A_BEGIN = ((0, (4,)), (2, (5,)), (5, (7,)))
-LEG1_BEGIN = 5
-LEG2_BEGIN = 8
-Z_BEGIN = 14
+FIRST = (1, 2)
+A_BEGIN = ((0, (3, 4)), (2, (5, 6)))
+LEG1_BEGIN = 4
+LEG2_BEGIN = 9
+Z_BEGIN = 12
 Z_END = STEPS + 2
 
 
@@ -220,7 +220,7 @@
         last(n, h).start()
 
     def ready(n, h):
-        return ORDER.index((1, 7)[n]) * PER + h + 4 <= Z_END
+        return max(ORDER.index((1, 7)[n]), FAR) * PER + h + 5 <= Z_END
 
     def stage1(i):
         p = lax.rem(i, RING)

time: 130 us -> 130 us (level)
  no operation moved by 1% of the time
where the time goes in v4:
time: 130 us; the launch traced here: 129 us
  Pallas kernels  128 us (98%)
  local copies, waits for them, and re-layouts  1.57 us (1%)
    pallas_call x1, Pallas kernels, update(): pl.pallas_call(ladder_kernel, out_shape=jax.ShapeDtypeStruct((ROWS, COLS)...  128 us

profile of v4, /device:TPU:2, one launch (start us, length us, event | category | flops | bytes accessed | tf_op | source)
XLA Modules:
  0.0 129.3 jit_solution(2543622253570575749)
XLA Ops:
  0.0 127.7 %ladder.1 = f32[256,128]{1,0:T(8,128)} custom-call(s32[8]{0:T(128)} %sizes_hbm.1, f32[256,3072]{1,0:T(8,128)} %a_hbm.1, f32[16,2,128,384]{3,2,1,0:T(8,128)} %bitcast.7, s32[1,256]{1,0:T(1,128)} %bitcast.9, s32[1,256]{1,0:T(1,128)} %bitcast.10, s32[1,128]{1,0:T(1,128)} %bitcast.11, s32[1,128]{1,0:T(1,128)} %bitcast.12, f32[1,100]{1,0:T(1,128)} %bitcast.13, ...), custom_call_target="tpu_custom_call" | custom-call | flops 19327352832 | bytes 12582912 | tf_op jit(solution)/shard_map/ladder/pallas_call | solution.py:422
  127.7 1.6 %copy.12 = f32[256,128]{1,0:T(8,128)} copy(f32[256,128]{1,0:T(8,128)} %ladder.1) | data formatting | bytes 262144

commit v5 on v4

--- a/solution.py
+++ b/solution.py
@@ -24,6 +24,12 @@
 RING = 4
 ORDER = (0, 1, 7, 2, 6, 3, 5, 4)
 FAR = ORDER.index(4)
+TABLE = [(0, h) for h in range(PER // 2)] + [(k, h) for k in range(1, NZ) for h in range(PER)]
+TABLE += [(0, h) for h in range(PER // 2, PER)]
+AT = {entry: i for i, entry in enumerate(TABLE)}
+PART_AT = [min(i for i, entry in enumerate(TABLE) if entry[1] == h) for h in range(PER)]
+BLOCK_AT = [i for i, entry in enumerate(TABLE) if i == 0 or TABLE[i - 1][0] != entry[0]]
+FETCH_AT = [AT[k, 0] - 1 for k in range(NZ)]
 FIRST = (1, 2)
 A_BEGIN = ((0, (3, 4)), (2, (5, 6)))
 LEG1_BEGIN = 4
@@ -188,8 +194,8 @@
     def zparts(k):
         return range(2 if k == FAR else 1)
 
-    def zsend(k, h, part_at):
-        d, i = ORDER[k], k * PER + h
+    def zsend(i, k, h, part_at):
+        d = ORDER[k]
         if d == 4:
             src, dst, dev = done.at[i, pl.ds(part_at * QUART, QUART)], mh.at[part_at, h], zdev(3 + 2 * part_at)
         elif d < 4:
@@ -198,37 +204,42 @@
             src, dst, dev = done.at[i], mg.at[1, 6 - d, h], zdev(d + 1)
         return remote(src, dst, zs.at[k, h, part_at], zq.at[k, h, part_at], dev)
 
+    def entry(i):
+        k = sum(jnp.where(i == at, block, 0) for at, (block, h) in enumerate(TABLE))
+        return k, sum(jnp.where(i == at, h, 0) for at, (block, h) in enumerate(TABLE))
+
     def zstart(i):
+        block, h = entry(i)
         for k, d in enumerate(ORDER):
             if d not in (0, 1, 7):
-                @pl.when(i // PER == k)
+                @pl.when(block == k)
                 def _():
                     for n in zparts(k):
-                        zsend(k, lax.rem(i, PER), n).start()
+                        zsend(i, k, h, n).start()
 
     def last(n, h):
-        i = ORDER.index((1, 7)[n]) * PER + h
+        i = AT[ORDER.index((1, 7)[n]), h]
         return remote(done.at[i], fin.at[n, h], es.at[n, h], eq.at[n, h], zdev((1, 7)[n]))
 
     def merge(n, h):
         for d in ((2, 3), (6, 5))[n]:
-            zsend(ORDER.index(d), h, 0).wait_recv()
-        zsend(FAR, h, n).wait_recv()
-        i = ORDER.index((1, 7)[n]) * PER + h
+            k = ORDER.index(d)
+            zsend(AT[k, h], k, h, 0).wait_recv()
+        zsend(AT[FAR, h], FAR, h, n).wait_recv()
+        i = AT[ORDER.index((1, 7)[n]), h]
         done[i] += mg[n, 0, h] + mg[n, 1, h]
         done[i, pl.ds(n * QUART, QUART)] += mh[n, h]
         last(n, h).start()
 
     def ready(n, h):
-        return max(ORDER.index((1, 7)[n]), FAR) * PER + h + 5 <= Z_END
+        return max(AT[ORDER.index((1, 7)[n]), h], AT[FAR, h]) + 5 <= Z_END
 
     def stage1(i):
         p = lax.rem(i, RING)
-        k = i // PER
-        h = lax.rem(i, PER)
+        k, h = entry(i)
 
         for step_at in range(PER):
-            @pl.when(i == step_at)
+            @pl.when(i == PART_AT[step_at])
             def _():
                 b_load(step_at).wait()
                 convert(b_own, step_at, 0, s)
@@ -237,9 +248,12 @@
                 b_swap(step_at).wait()
                 convert(b_sib, step_at, KD, slab(x, y, 1 - c))
 
-        @pl.when(h == 0)
+        @pl.when(functools.reduce(jnp.logical_or, [i == at for at in BLOCK_AT[:-1]]))
         def _():
             forward(k).wait_recv()
+
+        @pl.when(functools.reduce(jnp.logical_or, [i == at for at in BLOCK_AT]))
+        def _():
             for first, source in ((0, a_own), (KD, a_sib)):
                 hi, lo = split(source[k])
                 a3[:, pl.ds(first, KD)] = hi
@@ -271,20 +285,13 @@
             for half in range(2):
                 leg1(half).start()
 
-    def fetch(i):
-        k = i // PER
-
-        @pl.when(k + 1 != FAR)
-        def _():
-            a_wait = remote(a_own.at[k + 1], a_own.at[k + 1], as_.at[k + 1], ar.at[k + 1], sibling)
-            a_wait.wait_recv()
-
-        @pl.when(k + 1 == FAR)
-        def _():
+    def fetch(k):
+        if k == FAR:
             for half in range(2):
                 leg2(half).wait_recv()
-
-        forward(k + 1).start()
+        else:
+            a_send(k).wait_recv()
+        forward(k).start()
 
     def stage2(i):
         p = lax.rem(i, RING)
@@ -329,9 +336,12 @@
             zstart(i)
 
     def step(i, carry):
-        pl.when(jnp.logical_and(lax.rem(i, PER) == PER - 1, i < STEPS - PER))(functools.partial(fetch, i))
+        for k in range(2, NZ):
+            pl.when(i == FETCH_AT[k])(functools.partial(fetch, k))
         for lag, stage in enumerate((stage1, stage2, stage3, stage4, stage5)):
             pl.when(jnp.logical_and(i >= lag, i < STEPS + lag))(functools.partial(stage, i - lag))
+            if lag == 0:
+                pl.when(i == FETCH_AT[1])(functools.partial(fetch, 1))
 
         @pl.when(i == LEG2_BEGIN)
         def _():
@@ -345,7 +355,7 @@
                 zstart(j)
                 return carry
 
-            lax.fori_loop(PER, Z_BEGIN - 3, begin, 0)
+            lax.fori_loop(0, Z_BEGIN - 3, begin, 0)
 
         @pl.when(i == Z_END)
         def _():
@@ -367,7 +377,7 @@
         for n in range(2):
             last(n, h).wait_recv()
         cols = pl.ds(h * SUB, SUB)
-        ladder = (done[h] + (fin[0, h] + fin[1, h])).T
+        ladder = (done[AT[0, h]] + (fin[0, h] + fin[1, h])).T
         out[:, cols] = (drive[:, cols] + ladder) / denominator[:, cols]
     for n in range(2):
         for h in range(PER):
@@ -376,7 +386,7 @@
         if d not in (0, 1, 7):
             for h in range(PER):
                 for n in zparts(k):
-                    zsend(k, h, n).wait_send()
+                    zsend(AT[k, h], k, h, n).wait_send()
     a_swap.wait_send()
     for k in range(1, NZ):
         forward(k).wait_send()

time: 130 us -> 130 us (level)
  no operation moved by 1% of the time
where the time goes in v5:
time: 130 us
  Pallas kernels  128 us (98%)
  local copies, waits for them, and re-layouts  1.57 us (1%)
    pallas_call x1, Pallas kernels, update(): pl.pallas_call(ladder_kernel, out_shape=jax.ShapeDtypeStruct((ROWS, COLS)...  128 us

profile of v5, /device:TPU:2, one launch (start us, length us, event | category | flops | bytes accessed | tf_op | source)
XLA Modules:
  0.0 129.7 jit_solution(16503336610551985699)
XLA Ops:
  0.0 128.1 %ladder.1 = f32[256,128]{1,0:T(8,128)} custom-call(s32[8]{0:T(128)} %sizes_hbm.1, f32[256,3072]{1,0:T(8,128)} %a_hbm.1, f32[16,2,128,384]{3,2,1,0:T(8,128)} %bitcast.7, s32[1,256]{1,0:T(1,128)} %bitcast.9, s32[1,256]{1,0:T(1,128)} %bitcast.10, s32[1,128]{1,0:T(1,128)} %bitcast.11, s32[1,128]{1,0:T(1,128)} %bitcast.12, f32[1,100]{1,0:T(1,128)} %bitcast.13, ...), custom_call_target="tpu_custom_call" | custom-call | flops 19327352832 | bytes 12582912 | tf_op jit(solution)/shard_map/ladder/pallas_call | solution.py:432
  128.1 1.6 %copy.12 = f32[256,128]{1,0:T(8,128)} copy(f32[256,128]{1,0:T(8,128)} %ladder.1) | data formatting | bytes 262144

commit v6 on v5

--- a/solution.py
+++ b/solution.py
@@ -31,7 +31,8 @@
 BLOCK_AT = [i for i, entry in enumerate(TABLE) if i == 0 or TABLE[i - 1][0] != entry[0]]
 FETCH_AT = [AT[k, 0] - 1 for k in range(NZ)]
 FIRST = (1, 2)
-A_BEGIN = ((0, (3, 4)), (2, (5, 6)))
+SECOND = (3, 4)
+A_BEGIN = ((2, (5, 6)),)
 LEG1_BEGIN = 4
 LEG2_BEGIN = 9
 Z_BEGIN = 12
@@ -118,9 +119,6 @@
 
     for k in FIRST:
         a_send(k).start()
-    for h in range(1, PER):
-        b_swap(h).start()
-        b_load(h).start()
     drive_copy.start()
     small[0].wait()
 
@@ -245,8 +243,13 @@
                 convert(b_own, step_at, 0, s)
                 if step_at == 0:
                     a_loc.wait()
+                    for kk in SECOND:
+                        a_send(kk).start()
                 b_swap(step_at).wait()
                 convert(b_sib, step_at, KD, slab(x, y, 1 - c))
+                if step_at + 1 < PER:
+                    b_swap(step_at + 1).start()
+                    b_load(step_at + 1).start()
 
         @pl.when(functools.reduce(jnp.logical_or, [i == at for at in BLOCK_AT[:-1]]))
         def _():

time: 130 us -> 130 us (level)
  no operation moved by 1% of the time
where the time goes in v6:
time: 130 us
  Pallas kernels  128 us (98%)
  local copies, waits for them, and re-layouts  1.57 us (1%)
    pallas_call x1, Pallas kernels, update(): pl.pallas_call(ladder_kernel, out_shape=jax.ShapeDtypeStruct((ROWS, COLS)...  128 us

profile of v6, /device:TPU:2, one launch (start us, length us, event | category | flops | bytes accessed | tf_op | source)
XLA Modules:
  0.0 129.7 jit_solution(13992113448885214962)
XLA Ops:
  0.0 128.1 %ladder.1 = f32[256,128]{1,0:T(8,128)} custom-call(s32[8]{0:T(128)} %sizes_hbm.1, f32[256,3072]{1,0:T(8,128)} %a_hbm.1, f32[16,2,128,384]{3,2,1,0:T(8,128)} %bitcast.7, s32[1,256]{1,0:T(1,128)} %bitcast.9, s32[1,256]{1,0:T(1,128)} %bitcast.10, s32[1,128]{1,0:T(1,128)} %bitcast.11, s32[1,128]{1,0:T(1,128)} %bitcast.12, f32[1,100]{1,0:T(1,128)} %bitcast.13, ...), custom_call_target="tpu_custom_call" | custom-call | flops 19327352832 | bytes 12582912 | tf_op jit(solution)/shard_map/ladder/pallas_call | solution.py:435
  128.1 1.6 %copy.12 = f32[256,128]{1,0:T(8,128)} copy(f32[256,128]{1,0:T(8,128)} %ladder.1) | data formatting | bytes 262144

commit v7 on v6

--- a/solution.py
+++ b/solution.py
@@ -8,7 +8,7 @@
 from jax.sharding import PartitionSpec as P
 
 MESH = pl.DeviceIdType.MESH
-NT = (((1,), (1,)), ((), ()))
+NN = (((1,), (0,)), ((), ()))
 
 NZ = 8
 NX = 4
@@ -258,14 +258,14 @@
         @pl.when(functools.reduce(jnp.logical_or, [i == at for at in BLOCK_AT]))
         def _():
             for first, source in ((0, a_own), (KD, a_sib)):
-                hi, lo = split(source[k])
-                a3[:, pl.ds(first, KD)] = hi
-                a3[:, pl.ds(2 * KD + first, KD)] = hi
-                a3[:, pl.ds(4 * KD + first, KD)] = lo
+                hi, lo = split(source[k].T)
+                a3[pl.ds(first, KD), :] = hi
+                a3[pl.ds(2 * KD + first, KD), :] = hi
+                a3[pl.ds(4 * KD + first, KD), :] = lo
 
         def columns(m, carry):
             rows = pl.ds(pl.multiple_of(m * MROWS, MROWS), MROWS)
-            acc = lax.dot_general(b3[h, rows, :], a3[...], NT, preferred_element_type=jnp.float32)
+            acc = lax.dot_general(b3[h, rows, :], a3[...], NN, preferred_element_type=jnp.float32)
             for xx in range(2):
                 for yy in range(NX):
                     at = (xx * NX + yy) * SUB
@@ -414,7 +414,7 @@
         pltpu.VMEM((2, ROWS // 2, KD), f32),
         pltpu.VMEM((PER, NX * NX, SUB, KD), f32),
         pltpu.VMEM((PER, NX * NX, SUB, KD), f32),
-        pltpu.VMEM((ROWS, 6 * KD), bf16),
+        pltpu.VMEM((6 * KD, ROWS), bf16),
         pltpu.VMEM((PER, NX * NX * SUB, 6 * KD), bf16),
         pltpu.VMEM((RING, 2, NX, NX, SUB, LANES), f32),
         pltpu.VMEM((RING, 2, NX, SUB, LANES), f32),

time: 130 us -> 130 us (level)
  no operation moved by 1% of the time
where the time goes in v7:
time: 130 us; the launch traced here: 129 us
  Pallas kernels  128 us (98%)
  local copies, waits for them, and re-layouts  1.57 us (1%)
    pallas_call x1, Pallas kernels, update(): pl.pallas_call(ladder_kernel, out_shape=jax.ShapeDtypeStruct((ROWS, COLS)...  128 us

profile of v7, /device:TPU:2, one launch (start us, length us, event | category | flops | bytes accessed | tf_op | source)
XLA Modules:
  0.0 129.5 jit_solution(13901708954815911136)
XLA Ops:
  0.0 127.9 %ladder.1 = f32[256,128]{1,0:T(8,128)} custom-call(s32[8]{0:T(128)} %sizes_hbm.1, f32[256,3072]{1,0:T(8,128)} %a_hbm.1, f32[16,2,128,384]{3,2,1,0:T(8,128)} %bitcast.7, s32[1,256]{1,0:T(1,128)} %bitcast.9, s32[1,256]{1,0:T(1,128)} %bitcast.10, s32[1,128]{1,0:T(1,128)} %bitcast.11, s32[1,128]{1,0:T(1,128)} %bitcast.12, f32[1,100]{1,0:T(1,128)} %bitcast.13, ...), custom_call_target="tpu_custom_call" | custom-call | flops 19327352832 | bytes 12582912 | tf_op jit(solution)/shard_map/ladder/pallas_call | solution.py:435
  127.9 1.6 %copy.12 = f32[256,128]{1,0:T(8,128)} copy(f32[256,128]{1,0:T(8,128)} %ladder.1) | data formatting | bytes 262144

commit v8 on v6

--- a/solution.py
+++ b/solution.py
@@ -15,13 +15,17 @@
 ROWS = 256
 KD = 384
 COLS = 128
-SUB = 64
+SUB = 32
 PER = COLS // SUB
 QUART = SUB // 2
 STEPS = NZ * PER
 LANES = 128
-MROWS = 2 * NX * SUB
-RING = 4
+XS = 4
+MROWS = XS * NX * SUB
+RING = 8
+LAGS = (0, 2, 4)
+LAG = LAGS[2] + 1
+END = LAG + LAGS[2]
 ORDER = (0, 1, 7, 2, 6, 3, 5, 4)
 FAR = ORDER.index(4)
 TABLE = [(0, h) for h in range(PER // 2)] + [(k, h) for k in range(1, NZ) for h in range(PER)]
@@ -29,14 +33,14 @@
 AT = {entry: i for i, entry in enumerate(TABLE)}
 PART_AT = [min(i for i, entry in enumerate(TABLE) if entry[1] == h) for h in range(PER)]
 BLOCK_AT = [i for i, entry in enumerate(TABLE) if i == 0 or TABLE[i - 1][0] != entry[0]]
-FETCH_AT = [AT[k, 0] - 1 for k in range(NZ)]
+FETCH_AT = [AT[k, 0] - PER // 2 for k in range(NZ)]
 FIRST = (1, 2)
 SECOND = (3, 4)
-A_BEGIN = ((2, (5, 6)),)
-LEG1_BEGIN = 4
-LEG2_BEGIN = 9
-Z_BEGIN = 12
-Z_END = STEPS + 2
+A_BEGIN = ((4, (5, 6)),)
+LEG1_BEGIN = 8
+LEG2_BEGIN = 18
+Z_BEGIN = 27
+Z_END = STEPS + END - 2
 
 
 def split(v):
@@ -48,8 +52,8 @@
 def ladder_kernel(
     sizes_hbm, a_hbm, b_hbm, pf_hbm, ps_hbm, af_hbm, as_hbm, occ_hbm, virt_hbm, drive_hbm, out,
     drive, drive_sem, denominator, sizes, pf, ps, af, asec, occ, virt, small_sem, a_own, a_sib, relay, b_own, b_sib, a3, b3, part, quad, done,
-    r1, r2, r3, r4, mg, mh, fin,
-    loc_sem, bl, bs, br, as_, ar, hs, hr, fs, fr, s1, q1, s2, q2, s3, q3, s4, q4, zs, zq, es, eq,
+    o1, o2, r1, r2, mg, mh, fin,
+    loc_sem, bl, bs, br, as_, ar, hs, hr, fs, fr, s1, q1, s2, q2, zs, zq, es, eq,
 ):
     z = lax.axis_index("pair")
     s = lax.axis_index("slab")
@@ -96,11 +100,14 @@
     drive_copy = pltpu.make_async_copy(drive_hbm, drive, drive_sem)
     for copy in small:
         copy.start()
-    b_load(0).start()
+    for h in range(PER // 2):
+        b_load(h).start()
     a_loc.start()
     pl.semaphore_wait(barrier, len(peers))
     b_swap(0).start()
     a_swap.start()
+    for h in range(1, PER // 2):
+        b_swap(h).start()
 
     def a_send(k):
         d = NZ - ORDER[k]
@@ -159,35 +166,26 @@
 
         lax.fori_loop(0, NX * NX, one, 0)
 
-    def send1(i):
-        p = lax.rem(i, RING)
-        src = (
-            part.at[p, 0, xo, :, pl.ds(0, QUART)],
-            part.at[p, 0, xo, :, pl.ds(QUART, QUART)],
-            part.at[p, 1, :, yo, pl.ds(0, QUART)],
-            part.at[p, 1, :, yo, pl.ds(QUART, QUART)],
-        )
-        return [remote(src[k], r1.at[p, k], s1.at[p, k], q1.at[p, k], side[k]) for k in range(4)]
-
-    def send2(i):
-        p = lax.rem(i, RING)
-        src = (part.at[p, 0, xp], part.at[p, 0, xm], part.at[p, 1, :, yp], part.at[p, 1, :, ym])
-        return [remote(src[k], r2.at[p, k], s2.at[p, k], q2.at[p, k], side[k]) for k in range(4)]
-
-    def send3(i):
-        p = lax.rem(i, RING)
-        src = (
-            quad.at[p, 1, xo, pl.ds(0, QUART)],
-            quad.at[p, 1, xo, pl.ds(QUART, QUART)],
-            quad.at[p, 0, yo, pl.ds(0, QUART)],
-            quad.at[p, 0, yo, pl.ds(QUART, QUART)],
-        )
-        return [remote(src[k], r3.at[p, k], s3.at[p, k], q3.at[p, k], side[k]) for k in range(4)]
-
-    def send4(i):
-        p = lax.rem(i, RING)
-        src = (quad.at[p, 1, xp], quad.at[p, 1, xm], quad.at[p, 0, yp], quad.at[p, 0, ym])
-        return [remote(src[k], r4.at[p, k], s4.at[p, k], q4.at[p, k], side[k]) for k in range(4)]
+    def send1(j, whole):
+        p = lax.rem(j, RING)
+        at = (lambda ref, k: ref.at[p, k]) if whole else (lambda ref, k: ref.at[p, k, NX])
+        return [remote(at(o1, k), at(r1, k), s1.at[p, k], q1.at[p, k], side[k]) for k in range(4)]
+
+    def send2(j, whole):
+        p = lax.rem(j, RING)
+        at = (lambda ref, k: ref.at[p, k]) if whole else (lambda ref, k: ref.at[p, k, NX])
+        return [remote(at(o2, k), at(r2, k), s2.at[p, k], q2.at[p, k], side[k]) for k in range(4)]
+
+    def copies(send, j, act):
+        @pl.when(j < STEPS)
+        def _():
+            for copy in send(j, True):
+                act(copy)
+
+        @pl.when(j >= STEPS)
+        def _():
+            for copy in send(j, False):
+                act(copy)
 
     def zparts(k):
         return range(2 if k == FAR else 1)
@@ -230,9 +228,9 @@
         last(n, h).start()
 
     def ready(n, h):
-        return max(AT[ORDER.index((1, 7)[n]), h], AT[FAR, h]) + 5 <= Z_END
-
-    def stage1(i):
+        return max(AT[ORDER.index((1, 7)[n]), h], AT[FAR, h]) + END + 1 <= Z_END
+
+    def dots(i):
         p = lax.rem(i, RING)
         k, h = entry(i)
 
@@ -247,9 +245,9 @@
                         a_send(kk).start()
                 b_swap(step_at).wait()
                 convert(b_sib, step_at, KD, slab(x, y, 1 - c))
-                if step_at + 1 < PER:
-                    b_swap(step_at + 1).start()
-                    b_load(step_at + 1).start()
+                if step_at + PER // 2 < PER:
+                    b_swap(step_at + PER // 2).start()
+                    b_load(step_at + PER // 2).start()
 
         @pl.when(functools.reduce(jnp.logical_or, [i == at for at in BLOCK_AT[:-1]]))
         def _():
@@ -266,17 +264,33 @@
         def columns(m, carry):
             rows = pl.ds(pl.multiple_of(m * MROWS, MROWS), MROWS)
             acc = lax.dot_general(b3[h, rows, :], a3[...], NT, preferred_element_type=jnp.float32)
-            for xx in range(2):
+            for xx in range(XS):
                 for yy in range(NX):
                     at = (xx * NX + yy) * SUB
                     for half in range(2):
-                        part[p, half, 2 * m + xx, yy] = acc[at:at + SUB, half * LANES:(half + 1) * LANES]
+                        part[p, half, XS * m + xx, yy] = acc[at:at + SUB, half * LANES:(half + 1) * LANES]
             return carry
 
-        lax.fori_loop(0, NX // 2, columns, 0)
-        for copy in send1(i):
-            copy.start()
-
+        lax.fori_loop(0, NX // XS, columns, 0)
+        o1[p, 0, pl.ds(0, NX)] = part[p, 0, xo, :, pl.ds(0, QUART)]
+        o1[p, 1, pl.ds(0, NX)] = part[p, 0, xo, :, pl.ds(QUART, QUART)]
+        o1[p, 2, pl.ds(0, NX)] = part[p, 1, :, yo, pl.ds(0, QUART)]
+        o1[p, 3, pl.ds(0, NX)] = part[p, 1, :, yo, pl.ds(QUART, QUART)]
+
+    def boxes1(j):
+        p, old = lax.rem(j, RING), lax.rem(j + RING - LAG, RING)
+        pl.when(j < STEPS)(functools.partial(dots, j))
+
+        @pl.when(j >= LAG)
+        def _():
+            o1[p, 0, NX] = quad[old, 1, xo, pl.ds(0, QUART)]
+            o1[p, 1, NX] = quad[old, 1, xo, pl.ds(QUART, QUART)]
+            o1[p, 2, NX] = quad[old, 0, yo, pl.ds(0, QUART)]
+            o1[p, 3, NX] = quad[old, 0, yo, pl.ds(QUART, QUART)]
+
+        copies(send1, j, lambda copy: copy.start())
+
+    def begin_z(i):
         for begin, blocks in A_BEGIN:
             @pl.when(i == begin)
             def _():
@@ -296,54 +310,59 @@
             a_send(k).wait_recv()
         forward(k).start()
 
-    def stage2(i):
-        p = lax.rem(i, RING)
-        for copy in send1(i):
-            copy.wait()
-        part[p, 0, xp, :, pl.ds(0, QUART)] += r1[p, 0]
-        part[p, 0, xm, :, pl.ds(QUART, QUART)] += r1[p, 1]
-        part[p, 1, :, yp, pl.ds(0, QUART)] += r1[p, 2]
-        part[p, 1, :, ym, pl.ds(QUART, QUART)] += r1[p, 3]
-        for copy in send2(i):
-            copy.start()
-
-    def stage3(i):
-        p = lax.rem(i, RING)
-        for copy in send2(i):
-            copy.wait()
-        quad[p, 0] = part[p, 0, x] + (r2[p, 0] + r2[p, 1])
-        quad[p, 1] = part[p, 1, :, y] + (r2[p, 2] + r2[p, 3])
-        for copy in send3(i):
-            copy.start()
-
-    def stage4(i):
-        p = lax.rem(i, RING)
-        for copy in send3(i):
-            copy.wait()
-        quad[p, 1, xp, pl.ds(0, QUART)] += r3[p, 0]
-        quad[p, 1, xm, pl.ds(QUART, QUART)] += r3[p, 1]
-        quad[p, 0, yp, pl.ds(0, QUART)] += r3[p, 2]
-        quad[p, 0, ym, pl.ds(QUART, QUART)] += r3[p, 3]
-        for copy in send4(i):
-            copy.start()
-
-    def stage5(i):
-        p = lax.rem(i, RING)
-        for copy in send4(i):
-            copy.wait()
-        done[i, :, pl.ds(0, LANES)] = quad[p, 0, y] + (r4[p, 2] + r4[p, 3])
-        done[i, :, pl.ds(LANES, LANES)] = quad[p, 1, x] + (r4[p, 0] + r4[p, 1])
-
-        @pl.when(i > Z_BEGIN - 4)
-        def _():
-            zstart(i)
+    low, high = pl.ds(0, QUART), pl.ds(QUART, QUART)
+
+    def boxes2(j):
+        p, old = lax.rem(j, RING), lax.rem(j + RING - LAG, RING)
+        copies(send1, j, lambda copy: copy.wait())
+
+        @pl.when(j < STEPS)
+        def _():
+            n = pl.ds(0, NX)
+            o2[p, 0, n, low] = part[p, 0, xp, :, low] + r1[p, 0, n]
+            o2[p, 0, n, high] = part[p, 0, xp, :, high]
+            o2[p, 1, n, low] = part[p, 0, xm, :, low]
+            o2[p, 1, n, high] = part[p, 0, xm, :, high] + r1[p, 1, n]
+            o2[p, 2, n, low] = part[p, 1, :, yp, low] + r1[p, 2, n]
+            o2[p, 2, n, high] = part[p, 1, :, yp, high]
+            o2[p, 3, n, low] = part[p, 1, :, ym, low]
+            o2[p, 3, n, high] = part[p, 1, :, ym, high] + r1[p, 3, n]
+
+        @pl.when(j >= LAG)
+        def _():
+            for k, half, to in ((0, 1, xp), (1, 1, xm), (2, 0, yp), (3, 0, ym)):
+                plus, plain = (low, high) if k % 2 == 0 else (high, low)
+                o2[p, k, NX, plus] = quad[old, half, to, plus] + r1[p, k, NX]
+                o2[p, k, NX, plain] = quad[old, half, to, plain]
+
+        copies(send2, j, lambda copy: copy.start())
+
+    def sums(j):
+        p, old = lax.rem(j, RING), lax.rem(j + RING - LAG, RING)
+        copies(send2, j, lambda copy: copy.wait())
+
+        @pl.when(j < STEPS)
+        def _():
+            n = pl.ds(0, NX)
+            quad[p, 0] = part[p, 0, x] + (r2[p, 0, n] + r2[p, 1, n])
+            quad[p, 1] = part[p, 1, :, y] + (r2[p, 2, n] + r2[p, 3, n])
+
+        @pl.when(j >= LAG)
+        def _():
+            done[j - LAG, :, pl.ds(0, LANES)] = quad[old, 0, y] + (r2[p, 2, NX] + r2[p, 3, NX])
+            done[j - LAG, :, pl.ds(LANES, LANES)] = quad[old, 1, x] + (r2[p, 0, NX] + r2[p, 1, NX])
+
+            @pl.when(j - LAG > Z_BEGIN - END)
+            def _():
+                zstart(j - LAG)
 
     def step(i, carry):
         for k in range(2, NZ):
             pl.when(i == FETCH_AT[k])(functools.partial(fetch, k))
-        for lag, stage in enumerate((stage1, stage2, stage3, stage4, stage5)):
-            pl.when(jnp.logical_and(i >= lag, i < STEPS + lag))(functools.partial(stage, i - lag))
+        for lag, stage in zip(LAGS, (boxes1, boxes2, sums)):
+            pl.when(jnp.logical_and(i >= lag, i < STEPS + LAG + lag))(functools.partial(stage, i - lag))
             if lag == 0:
+                begin_z(i)
                 pl.when(i == FETCH_AT[1])(functools.partial(fetch, 1))
 
         @pl.when(i == LEG2_BEGIN)
@@ -358,7 +377,7 @@
                 zstart(j)
                 return carry
 
-            lax.fori_loop(0, Z_BEGIN - 3, begin, 0)
+            lax.fori_loop(0, Z_BEGIN - END + 1, begin, 0)
 
         @pl.when(i == Z_END)
         def _():
@@ -369,7 +388,7 @@
 
         return carry
 
-    lax.fori_loop(0, STEPS + 4, step, 0)
+    lax.fori_loop(0, STEPS + END, step, 0)
 
     for n in range(2):
         for h in range(PER):
@@ -419,16 +438,15 @@
         pltpu.VMEM((RING, 2, NX, NX, SUB, LANES), f32),
         pltpu.VMEM((RING, 2, NX, SUB, LANES), f32),
         pltpu.VMEM((STEPS, SUB, ROWS), f32),
-        pltpu.VMEM((RING, 4, NX, QUART, LANES), f32),
-        pltpu.VMEM((RING, 4, NX, SUB, LANES), f32),
-        pltpu.VMEM((RING, 4, QUART, LANES), f32),
-        pltpu.VMEM((RING, 4, SUB, LANES), f32),
+        pltpu.VMEM((RING, 4, NX + 1, QUART, LANES), f32),
+        pltpu.VMEM((RING, 4, NX + 1, SUB, LANES), f32),
+        pltpu.VMEM((RING, 4, NX + 1, QUART, LANES), f32),
+        pltpu.VMEM((RING, 4, NX + 1, SUB, LANES), f32),
         pltpu.VMEM((2, 2, PER, SUB, ROWS), f32),
         pltpu.VMEM((2, PER, QUART, ROWS), f32),
         pltpu.VMEM((2, PER, SUB, ROWS), f32),
         dma, dma((PER,)), dma((PER,)), dma((PER,)),
         dma((NZ,)), dma((NZ,)), dma((4,)), dma((4,)), dma((NZ,)), dma((NZ,)),
-        dma((RING, 4)), dma((RING, 4)), dma((RING, 4)), dma((RING, 4)),
         dma((RING, 4)), dma((RING, 4)), dma((RING, 4)), dma((RING, 4)),
         dma((NZ, PER, 2)), dma((NZ, PER, 2)), dma((2, PER)), dma((2, PER)),
     ]

time: 130 us -> 131 us (level)
  no operation moved by 1% of the time
where the time goes in v8:
time: 131 us
  Pallas kernels  129 us (98%)
  local copies, waits for them, and re-layouts  1.57 us (1%)
    pallas_call x1, Pallas kernels, update(): pl.pallas_call(ladder_kernel, out_shape=jax.ShapeDtypeStruct((ROWS, COLS)...  129 us

profile of v8, /device:TPU:2, one launch (start us, length us, event | category | flops | bytes accessed | tf_op | source)
XLA Modules:
  0.0 130.5 jit_solution(15541002979603885636)
XLA Ops:
  0.0 128.9 %ladder.1 = f32[256,128]{1,0:T(8,128)} custom-call(s32[8]{0:T(128)} %sizes_hbm.1, f32[256,3072]{1,0:T(8,128)} %a_hbm.1, f32[16,2,128,384]{3,2,1,0:T(8,128)} %bitcast.7, s32[1,256]{1,0:T(1,128)} %bitcast.9, s32[1,256]{1,0:T(1,128)} %bitcast.10, s32[1,128]{1,0:T(1,128)} %bitcast.11, s32[1,128]{1,0:T(1,128)} %bitcast.12, f32[1,100]{1,0:T(1,128)} %bitcast.13, ...), custom_call_target="tpu_custom_call" | custom-call | flops 19327352832 | bytes 12582912 | tf_op jit(solution)/shard_map/ladder/pallas_call | solution.py:453
  128.9 1.6 %copy.12 = f32[256,128]{1,0:T(8,128)} copy(f32[256,128]{1,0:T(8,128)} %ladder.1) | data formatting | bytes 262144

commit v9 on v4

--- a/solution.py
+++ b/solution.py
@@ -25,10 +25,10 @@
 ORDER = (0, 1, 7, 2, 6, 3, 5, 4)
 FAR = ORDER.index(4)
 FIRST = (1, 2)
-A_BEGIN = ((0, (3, 4)), (2, (5, 6)))
-LEG1_BEGIN = 4
-LEG2_BEGIN = 9
-Z_BEGIN = 12
+A_BEGIN = ((0, (3, 4)), (3, (5, 6)))
+LEG1_BEGIN = 8
+LEG2_BEGIN = 11
+Z_BEGIN = 14
 Z_END = STEPS + 2
 
 

time: 130 us -> 129 us (level)
  no operation moved by 1% of the time
where the time goes in v9:
time: 129 us; the launch traced here: 128 us
  Pallas kernels  127 us (98%)
  local copies, waits for them, and re-layouts  1.57 us (1%)
    pallas_call x1, Pallas kernels, update(): pl.pallas_call(ladder_kernel, out_shape=jax.ShapeDtypeStruct((ROWS, COLS)...  127 us

profile of v9, /device:TPU:2, one launch (start us, length us, event | category | flops | bytes accessed | tf_op | source)
XLA Modules:
  0.0 128.5 jit_solution(1578155262954536531)
XLA Ops:
  0.0 126.9 %ladder.1 = f32[256,128]{1,0:T(8,128)} custom-call(s32[8]{0:T(128)} %sizes_hbm.1, f32[256,3072]{1,0:T(8,128)} %a_hbm.1, f32[16,2,128,384]{3,2,1,0:T(8,128)} %bitcast.7, s32[1,256]{1,0:T(1,128)} %bitcast.9, s32[1,256]{1,0:T(1,128)} %bitcast.10, s32[1,128]{1,0:T(1,128)} %bitcast.11, s32[1,128]{1,0:T(1,128)} %bitcast.12, f32[1,100]{1,0:T(1,128)} %bitcast.13, ...), custom_call_target="tpu_custom_call" | custom-call | flops 19327352832 | bytes 12582912 | tf_op jit(solution)/shard_map/ladder/pallas_call | solution.py:422
  126.9 1.6 %copy.12 = f32[256,128]{1,0:T(8,128)} copy(f32[256,128]{1,0:T(8,128)} %ladder.1) | data formatting | bytes 262144
